TPU v7x, 256 devices: a whole 4x4x8 slice. The times are simulated.
256 devices in a mesh: dp: 64 (over z_lo, x, y, core), tensor: 4 (over z_hi).
Axes of the slice: x: 4, y: 4, z: 8 (z_hi: 4, z_lo: 2; z = z_hi * 2 + z_lo), core: 2. Of those that a mesh axis runs over, the one named last changes fastest.
Arguments:
- inputs: bfloat16 [40960, 8192], P(('dp', 'tensor')), may hold values from -6 to 6
- kv_grads: bfloat16 [2, 40960, 512], P(None, 'dp', 'tensor'), may hold values from -0.03125 to 0.03125
- error: bfloat16 [2, 64, 8192, 512], P(None, 'dp', None, 'tensor'), may hold values from -2 to 2
- q_init: float32 [2, 512, 32], P(None, 'tensor'), may hold values from -6 to 6
Outputs:
- p_factor: float32 [2, 8192, 128], P(None, 'dp', 'tensor')
- q_factor: float32 [2, 512, 32], P(None, 'tensor')
- new_error: bfloat16 [2, 64, 8192, 512], P(None, 'dp', None, 'tensor')
All inputs are finite; a program needn't handle non-finite values.
Results may differ from a plain program's by a relative error of at most 0.0044.
Values may be sent and summed in bfloat16 or wider, within the bound.
A program may use at most 128 MiB of HBM per device.

v0:
```python
import jax
import jax.numpy as jnp
from jax import lax
from jax.sharding import PartitionSpec as P


def orthonormal(matrix):

    def add_column(column_index, columns_done):
        position = jnp.asarray(column_index).astype(jnp.int32)
        vector = lax.dynamic_slice_in_dim(matrix, position, 1, 1)
        coeffs = jnp.dot(columns_done.T, vector, precision=lax.Precision.HIGHEST)
        vector = vector - jnp.dot(columns_done, coeffs, precision=lax.Precision.HIGHEST)
        vector = vector / jnp.sqrt(jnp.sum(vector * vector))
        return lax.dynamic_update_slice_in_dim(columns_done, vector, position, 1)

    return lax.fori_loop(0, matrix.shape[1], add_column, jnp.zeros_like(matrix))


def local(inputs, kv_grads, error, q_init):
    model_width = inputs.shape[1]
    replicas = lax.axis_size("dp")
    share_rows = model_width // replicas
    gradient = jnp.einsum(
        "nd,wnc->wdc",
        lax.all_gather(inputs, "tensor", axis=0, tiled=True),
        kv_grads,
        preferred_element_type=jnp.float32,
    )
    merged = gradient + error[:, 0].astype(jnp.float32)
    factor = jnp.einsum("wdc,wck->wdk", merged, q_init, precision=lax.Precision.HIGHEST)
    summed_factor = lax.psum(factor, "dp")
    full_basis = jax.vmap(orthonormal)(summed_factor)
    own_rows = lax.dynamic_slice_in_dim(
        full_basis, lax.axis_index("dp") * share_rows, share_rows, 1
    )
    projected = jnp.einsum("wdc,wdk->wck", merged, full_basis, precision=lax.Precision.HIGHEST)
    q_factor = lax.psum(projected, "dp")
    update = (
        jnp.einsum("wdk,wck->wdc", full_basis, q_factor, precision=lax.Precision.HIGHEST) / replicas
    )
    new_error = (merged - update).astype(jnp.bfloat16)[:, None]
    return (own_rows, q_factor, new_error)


def solution(mesh):
    in_specs = (
        P(("dp", "tensor"), None),
        P(None, "dp", "tensor"),
        P(None, "dp", None, "tensor"),
        P(None, "tensor", None),
    )
    out_specs = (P(None, "dp", "tensor"), P(None, "tensor", None), P(None, "dp", None, "tensor"))
    return jax.shard_map(local, mesh=mesh, in_specs=in_specs, out_specs=out_specs, check_vma=False)
```

profile of v0, /device:TPU:1, one launch (start us, length us, event | category | flops | bytes accessed | tf_op | source)
XLA Modules:
  0.0 1426.0 jit_solution(7293203543265621760)
XLA Ops:
  8.0 6.3 copy.18
  14.3 187.9 %all-gather.2.cloned.1.call-done = bf16[640,8192]{1,0:T(8,128)(2,1)} async-done(((bf16[160,8192]{1,0:T(8,128)(2,1)}), bf16[640,8192]{1,0:T(8,128)(2,1)}) %all-gather.2.cloned.1.call-update) | async-done | bytes 10485776 | tf_op jit(solution)/shard_map/all_gather | solution.py:26
  202.2 8.6 fusion.12
  210.8 3.2 copy-done.1
  214.0 6.0 fusion.20
  220.1 555.6 %all-reduce.2.cloned.1.call-done = f32[2,8192,32]{1,2,0:T(8,128)} async-done(((f32[2,8192,32]{1,2,0:T(8,128)}), f32[2,8192,32]{1,2,0:T(8,128)}) %all-reduce.2.cloned.1.call-update) | async-done | bytes 2097168 | tf_op jit(solution)/shard_map/psum | solution.py:32
  776.7 336.2 %while.15 = (s32[]{:T(128)}, f32[2,8192,32]{1,0,2:T(2,128)S(1)}, f32[2,8192,32]{1,2,0:T(8,128)}, s32[]{:T(128)}, s32[1]{0:T(128)}, /*index=5*/s32[3]{0:T(128)S(1)}) while((s32[]{:T(128)}, f32[2,8192,32]{1,0,2:T(2,128)S(1)}, f32[2,8192,32]{1,2,0:T(8,128)}, s32[]{:T(128)}, s32[1]{0:T(128)}, /*index=5*/s32[3]{0:T(128)S(1)}) %tuple.56), condition=%wide.region_4.0_spmd, body=%wide.region_1.0_spmd.sunk | while | flops 12681238 | bytes 4850863 | solution.py:17
  779.3 2.8 fusion.41
  789.8 2.8 fusion.41
  800.3 2.8 fusion.41
  810.8 2.8 fusion.41
  821.3 2.8 fusion.41
  831.8 2.8 fusion.41
  842.3 2.8 fusion.41
  852.8 2.8 fusion.41
  863.3 2.8 fusion.41
  873.8 2.8 fusion.41
  884.3 2.8 fusion.41
  894.8 2.8 fusion.41
  905.3 2.8 fusion.41
  915.8 2.8 fusion.41
  926.3 2.8 fusion.41
  936.8 2.8 fusion.41
  947.3 2.8 fusion.41
  957.8 2.8 fusion.41
  968.3 2.8 fusion.41
  978.8 2.8 fusion.41
  989.3 2.8 fusion.41
  1112.9 10.2 fusion.18
  1125.7 275.1 %psum.15 = f32[2,128,32]{1,2,0:T(8,128)S(1)} all-reduce(f32[2,128,32]{1,2,0:T(8,128)S(1)} %fusion.18), channel_id=1, replica_groups=mesh['dp'=64,'tensor'=4] {'dp'}, use_global_device_ids=true, to_apply=%region_5.0 | all-reduce | flops 8192 | bytes 65536 | tf_op jit(solution)/shard_map/psum | solution.py:38
  1400.7 10.8 fusion.16
  1411.5 6.3 copy.26
  (347 shorter events, 281.2 us)
Async XLA Ops:
  7.2 195.0 %copy-start = (bf16[2,640,128]{2,1,0:T(8,128)(2,1)S(1)}, bf16[2,640,128]{2,1,0:T(8,128)(2,1)}, u32[]{:S(2)}) copy-start(bf16[2,640,128]{2,1,0:T(8,128)(2,1)} %param.9) | copy-start | bytes 983044
  7.2 195.0 %all-gather.2.cloned.1.call-start = ((), (), s32[]{:S(2)}) async-start(), calls=%async_computation | async-start | bytes 13107200 | tf_op jit(solution)/shard_map/all_gather | solution.py:26
  7.9 767.8 %all-reduce.2.cloned.1.call-start = ((), (), s32[]{:S(2)}) async-start(), calls=%async_computation.1 | async-start | bytes 4194304 | tf_op jit(solution)/shard_map/psum | solution.py:32
  14.3 199.7 %copy-start.3 = (f32[2,128,32]{1,2,0:T(8,128)S(1)}, f32[2,128,32]{1,2,0:T(8,128)}, u32[]{:S(2)}) copy-start(f32[2,128,32]{1,2,0:T(8,128)} %param.11) | copy-start | bytes 98308
  210.8 3.2 copy-start.1
  220.1 556.6 %copy-start.4 = (s32[3]{0:T(128)S(1)}, s32[3]{0:T(128)}, u32[]{:S(2)}) copy-start(s32[3]{0:T(128)} %constant.89.clone.1) | copy-start | bytes 40
  1400.7 10.8 copy-start.2
Sparse Core Ops, SparseCore 0:
  9.8 192.2 all-gather.1
  220.2 555.4 all-reduce.1
where the time goes:
time: 1430 us
  waiting for transfers between devices  744 us (52%)
  blocking collectives  275 us (19%)
  matrix products  198 us (14%)
  local copies, waits for them, and re-layouts  114 us (8%)
  other arithmetic  79.5 us (6%)
    psum x1, waiting for transfers between devices, local(): summed_factor = lax.psum(factor, 'dp')  556 us
    psum x1, blocking collectives, local(): q_factor = lax.psum(projected, 'dp')  275 us
    all_gather x1, waiting for transfers between devices, local(): lax.all_gather(inputs, 'tensor', axis=0, tiled=True)  188 us
    dot_general x32, matrix products, add_column(): coeffs = jnp.dot(columns_done.T, vector, precision=lax.Precision.HIGHEST)  90.8 us
    dot_general x32, matrix products, add_column(): jnp.dot(columns_done, coeffs, precision=lax.Precision.HIGHEST)  71.6 us
    gather x32, local copies, waits for them, and re-layouts, add_column(): vector = lax.dynamic_slice_in_dim(matrix, position, 1, 1)  55.6 us
    scatter x32, other arithmetic, add_column(): return lax.dynamic_update_slice_in_dim(columns_done, vector, position, 1)  45.3 us
  transfers between devices with their start and end apart: 2, of which 2 were waited for; matrix products, arithmetic and copies ran while one was open for 0% of the time, Pallas kernels for 0%

commit v1 on v0

v1 whole, which is shorter than its diff:
```python
import functools

import jax
import jax.numpy as jnp
from jax import lax
from jax.experimental import pallas as pl
from jax.experimental.pallas import tpu as pltpu
from jax.sharding import PartitionSpec as P

MESH = pl.DeviceIdType.MESH
F32 = jnp.float32
BF16 = jnp.bfloat16
HIGHEST = lax.Precision.HIGHEST

D = 8192
HALF = 4096
TOK = 160
TILE = 512


def nt(a, b, precision=None):
    return lax.dot_general(
        a, b, (((1,), (1,)), ((), ())), preferred_element_type=F32, precision=precision
    )


def tn(a, b):
    return lax.dot_general(a, b, (((0,), (0,)), ((), ())), preferred_element_type=F32)


def nn(a, b, precision=None):
    return jnp.dot(a, b, preferred_element_type=F32, precision=precision)


def parts3(a):
    hi = a.astype(BF16)
    rest = a - hi.astype(F32)
    mid = rest.astype(BF16)
    low = (rest - mid.astype(F32)).astype(BF16)
    return hi, mid, low


def stacked3(a):
    return jnp.concatenate(parts3(a), axis=0)


def sum3(r):
    n = r.shape[0] // 3
    return (r[2 * n :] + r[n : 2 * n]) + r[:n]


def whitener(gram):
    rows = lax.broadcasted_iota(jnp.int32, (2, 32, 64), 1)
    cols = lax.broadcasted_iota(jnp.int32, (2, 32, 64), 2)
    eye = jnp.where(
        lax.broadcasted_iota(jnp.int32, (32, 32), 0) == lax.broadcasted_iota(jnp.int32, (32, 32), 1), 1.0, 0.0
    ).astype(F32)
    a = jnp.stack(
        [
            jnp.concatenate([gram[:32, :32], eye], axis=1),
            jnp.concatenate([gram[32:, 32:], eye], axis=1),
        ]
    )
    for j in range(31):
        scale = a[:, :, j : j + 1] / a[:, j : j + 1, j : j + 1]
        a = a - jnp.where(rows > j, scale * a[:, j : j + 1, :], 0.0)
    pivots = jnp.sum(jnp.where(rows == cols, a, 0.0), axis=2, keepdims=True)
    w = a[:, :, 32:] * (1.0 / jnp.sqrt(pivots))
    zero = jnp.zeros((32, 32), F32)
    return jnp.concatenate(
        [jnp.concatenate([w[0], zero], axis=1), jnp.concatenate([zero, w[1]], axis=1)], axis=0
    )


def kernel(
    x_ref, k_ref, e_ref, q_ref, p_out, q_out, ne_ref,
    xs, k2, ks, kr, kl, fo, fp, rc, ra, rb, a1, b1, ra2, rb2, ab, rz, fab, ga, gb, ft, b3, bt, ev, g,
    qc, qy, qx, qz, send_sem, recv_sem, local_sem, out_sem,
):
    t = lax.axis_index("tensor")
    dp = lax.axis_index("dp")
    c = lax.rem(dp, 2)
    yi = lax.rem(lax.div(dp, 2), 4)
    xi = lax.rem(lax.div(dp, 8), 4)
    zl = lax.div(dp, 32)
    zi = 2 * t + zl

    def device(x=xi, y=yi, z=zi, core=c):
        return {"dp": lax.rem(z, 2) * 32 + x * 8 + y * 2 + core, "tensor": lax.div(z, 2)}

    other_core = device(core=1 - c)
    x_peer = [None] + [device(x=lax.rem(xi + o, 4)) for o in (1, 2, 3)]
    y_peer = [None] + [device(y=lax.rem(yi + o, 4)) for o in (1, 2, 3)]
    z_peer = [None] + [device(z=lax.rem(zi + o, 8)) for o in range(1, 8)]
    other_zl = {"dp": lax.rem(dp + 32, 64), "tensor": t}
    t_right, t_left = z_peer[2], z_peer[6]

    started = []

    def send(src, dst, where):
        i = len(started)
        copy = pltpu.make_async_remote_copy(
            src_ref=src, dst_ref=dst, send_sem=send_sem.at[i], recv_sem=recv_sem.at[i],
            device_id=where, device_id_type=MESH,
        )
        copy.start()
        started.append(copy)
        return copy

    load_x = pltpu.make_async_copy(x_ref, xs.at[0], local_sem.at[0])
    load_e = pltpu.make_async_copy(e_ref, ev, local_sem.at[1])
    load_x.start()
    load_e.start()

    barrier = pltpu.get_barrier_semaphore()
    peers = [other_core] + x_peer[1:] + y_peer[1:] + z_peer[1:]
    for peer in peers:
        pl.semaphore_signal(barrier, inc=1, device_id=peer, device_id_type=MESH)

    ks[...] = jnp.zeros_like(ks)
    for w in range(2):
        q3 = stacked3(q_ref[w])
        k2[:, w * 128 : (w + 1) * 128] = k_ref[w]
        for s in range(4):
            ks[s, w * 32 : (w + 1) * 32, 0:TOK] = sum3(nt(q3, k_ref[w, s * TOK : (s + 1) * TOK, :]))

    pl.semaphore_wait(barrier, len(peers))

    kq = [send(ks.at[lax.rem(t + o, 4)], kr.at[t], z_peer[2 * o]) for o in (1, 2, 3)]
    kr[t] = ks[t]

    def rows(slot, start, size):
        return xs.at[slot, pl.ds(start, size)]

    def token_pair(to_right, to_left):
        (a, m), (b, n) = to_right, to_left
        return (
            send(x_ref.at[pl.ds(a, m)], rows(1, a, m), t_right),
            send(x_ref.at[pl.ds(b, n)], rows(2, b, n), t_left),
        )

    first = token_pair((0, 80), (80, 80))
    second = token_pair((80, 48), (0, 48))

    load_x.wait()
    for copy in kq:
        copy.wait_recv()
    hi, mid, low = parts3(kr[...].reshape(256, 256)[:, :TOK])
    kl[0:256] = hi
    kl[256:512] = mid
    kl[512:768] = low

    load_e.wait()
    q3s = [stacked3(q_ref[w]) for w in range(2)]

    def factor_tile(ref, at, there):
        at = pl.ds(at, TILE)
        ref[:, at] = sum3(nn(kl[...], xs[0, :, pl.ds(there, TILE)]))
        for w in range(2):
            mine = pl.ds(pl.multiple_of(t * 64 + w * 32, 32), 32)
            ref[mine, at] += sum3(nt(q3s[w], ev[w, pl.ds(there, TILE), :]))

    core_copies = []
    for piece in range(2):

        def partner_tile(i, carry, piece=piece):
            at = pl.multiple_of(piece * 2048 + i * TILE, TILE)
            factor_tile(fp, at, pl.multiple_of((1 - c) * HALF + at, TILE))
            return carry

        lax.fori_loop(0, 4, partner_tile, 0)
        part = pl.ds(piece * 2048, 2048)
        core_copies.append(send(fp.at[:, part], rc.at[:, part], other_core))

    def own_tile(i, carry):
        at = pl.multiple_of(i * TILE, TILE)
        factor_tile(fo, at, pl.multiple_of(c * HALF + at, TILE))
        return carry

    lax.fori_loop(0, 8, own_tile, 0)

    for copy in core_copies:
        copy.wait_recv()

    def add_core(start):
        def some_rows(i, carry):
            r = pl.ds(pl.multiple_of(i * 32, 32), 32)
            fo[r, pl.ds(start, TILE)] += rc[r, pl.ds(start, TILE)]
            return carry

        lax.fori_loop(0, 8, some_rows, 0)

    step1 = []
    for o in (2, 1, 3, 0):
        at_x = pl.multiple_of(lax.rem(xi + o, 4) * TILE, TILE)
        at_y = pl.multiple_of(2048 + lax.rem(yi + o, 4) * TILE, TILE)
        add_core(at_x)
        if o:
            step1.append(send(fo.at[:, pl.ds(at_x, TILE)], ra.at[o - 1], x_peer[o]))
        add_core(at_y)
        if o:
            step1.append(send(fo.at[:, pl.ds(at_y, TILE)], rb.at[o - 1], y_peer[o]))

    def grad_add(slot, start, size, owner, fresh=False):
        k = k2[pl.ds(pl.multiple_of(owner * TOK + start, 16), size), :]

        def tile(i, carry):
            at = pl.ds(pl.multiple_of(i * TILE, TILE), TILE)
            more = tn(xs[slot, start : start + size, at], k)
            if fresh:
                g[at, :] = more
            else:
                g[at, :] += more
            return carry

        lax.fori_loop(0, D // TILE, tile, 0)

    grad_add(0, 0, TOK, t, fresh=True)

    for copy in step1:
        copy.wait_recv()

    at_x = pl.multiple_of(xi * TILE, TILE)
    at_y = pl.multiple_of(2048 + yi * TILE, TILE)

    def sum_step1(i, carry):
        r = pl.ds(pl.multiple_of(i * 32, 32), 32)
        a1[r, :] = ((fo[r, pl.ds(at_x, TILE)] + ra[0, r, :]) + ra[1, r, :]) + ra[2, r, :]
        b1[r, :] = ((fo[r, pl.ds(at_y, TILE)] + rb[0, r, :]) + rb[1, r, :]) + rb[2, r, :]
        return carry

    lax.fori_loop(0, 8, sum_step1, 0)

    step2 = []
    for o in (2, 1, 3):
        to_y = pl.ds(pl.multiple_of(lax.rem(yi + o, 4) * 128, 128), 128)
        to_x = pl.ds(pl.multiple_of(lax.rem(xi + o, 4) * 128, 128), 128)
        step2.append(send(a1.at[:, to_y], ra2.at[o - 1], y_peer[o]))
        step2.append(send(b1.at[:, to_x], rb2.at[o - 1], x_peer[o]))
    for copy in step2:
        copy.wait_recv()
    at_y = pl.ds(pl.multiple_of(yi * 128, 128), 128)
    at_x = pl.ds(pl.multiple_of(xi * 128, 128), 128)
    ab[0] = ((a1[:, at_y] + ra2[0]) + ra2[1]) + ra2[2]
    ab[1] = ((b1[:, at_x] + rb2[0]) + rb2[1]) + rb2[2]

    step3 = []
    for o in (4, 3, 5, 2, 6, 1, 7):
        z = lax.rem(zi + o, 8)
        mine = pl.ds(pl.multiple_of(lax.div(z, 2) * 64, 64), 64)
        step3.append(send(ab.at[lax.rem(z, 2), mine], rz.at[o - 1], z_peer[o]))
    third = token_pair((128, 32), (48, 32))
    for copy in step3:
        copy.wait_recv()
    total = ab[zl, pl.ds(pl.multiple_of(t * 64, 64), 64), :]
    for o in range(7):
        total = total + rz[o]
    fab[zl] = total
    pair = send(fab.at[zl], fab.at[zl], other_zl)

    for copy in first:
        copy.wait_recv()
    forwards = []
    for a, b, n in ((0, 80, 48), (48, 128, 32)):
        forwards.append(
            (
                send(rows(1, a, n), rows(3, a, n), t_right),
                send(rows(2, b, n), rows(3, b, n), t_left),
            )
        )
    left, right, far = lax.rem(t + 3, 4), lax.rem(t + 1, 4), lax.rem(t + 2, 4)
    grad_add(1, 0, 80, left)
    grad_add(2, 80, 80, right)

    pair.wait_recv()
    step4 = []
    for o in (2, 1, 3):
        step4.append(send(fab.at[0], ga.at[:, at_y], y_peer[o]))
        step4.append(send(fab.at[1], gb.at[:, at_x], x_peer[o]))
    ga[:, at_y] = fab[0]
    gb[:, at_x] = fab[1]
    for copy in step4:
        copy.wait_recv()
    own_a = pl.ds(pl.multiple_of(c * HALF + xi * TILE, TILE), TILE)
    own_b = pl.ds(pl.multiple_of(c * HALF + 2048 + yi * TILE, TILE), TILE)
    step5 = []
    for o in (2, 1, 3):
        step5.append(send(ga, ft.at[:, own_a], x_peer[o]))
        step5.append(send(gb, ft.at[:, own_b], y_peer[o]))
    ft[:, own_a] = ga[...]
    ft[:, own_b] = gb[...]
    for copy in step5:
        copy.wait_recv()
    own_half = pl.ds(pl.multiple_of(c * HALF, HALF), HALF)
    step6 = send(ft.at[:, own_half], ft.at[:, own_half], other_core)
    step6.wait()

    def tile_at(i):
        return pl.ds(pl.multiple_of(i * TILE, TILE), TILE)

    def gram_tile(i, acc):
        f = ft[:, tile_at(i)]
        return acc + nt(f, f, HIGHEST)

    gram = lax.fori_loop(0, D // TILE, gram_tile, jnp.zeros((64, 64), F32))
    w1 = whitener(gram)

    def first_round(i, acc):
        b = nn(w1, ft[:, tile_at(i)], HIGHEST)
        ft[:, tile_at(i)] = b
        return acc + nt(b, b, HIGHEST)

    gram = lax.fori_loop(0, D // TILE, first_round, jnp.zeros((64, 64), F32))
    w2 = whitener(gram)

    def second_round(i, carry):
        b = nn(w2, ft[:, tile_at(i)], HIGHEST)
        ft[:, tile_at(i)] = b
        hi, mid, low = parts3(b)
        b3[0:64, tile_at(i)] = hi
        b3[64:128, tile_at(i)] = mid
        b3[128:192, tile_at(i)] = low
        both = jnp.concatenate([b, b - hi.astype(F32)], axis=0)
        bt[tile_at(i), :] = both.T.astype(BF16)
        return carry

    lax.fori_loop(0, D // TILE, second_round, 0)
    mine = pl.ds(pl.multiple_of(dp * 128, 128), 128)
    for w in range(2):
        p_out[w] = ft[w * 32 : (w + 1) * 32, mine]

    def error_tile(i, acc):
        b = b3[:, tile_at(i)]
        return tuple(acc[w] + nn(b, ev[w, tile_at(i), :]) for w in range(2))

    zero = jnp.zeros((192, 128), F32)
    by_w = lax.fori_loop(0, D // TILE, error_tile, (zero, zero))
    q_sum = [sum3(by_w[w])[w * 32 : (w + 1) * 32] for w in range(2)]

    def project(q_sum, slot, start, size, owner):
        def tile(i, acc):
            return acc + nt(b3[:, tile_at(i)], xs[slot, start : start + size, tile_at(i)])

        z = sum3(lax.fori_loop(0, D // TILE, tile, jnp.zeros((192, size), F32)))
        at = pl.ds(pl.multiple_of(owner * TOK + start, 16), size)
        return [
            q_sum[w] + sum3(nn(stacked3(z[w * 32 : (w + 1) * 32]), k_ref[w, at, :])) for w in range(2)
        ]

    q_sum = project(q_sum, 0, 0, TOK, t)
    q_sum = project(q_sum, 1, 0, 80, left)
    q_sum = project(q_sum, 2, 80, 80, right)
    for copy in second + third:
        copy.wait_recv()
    grad_add(1, 80, 80, left)
    grad_add(2, 0, 80, right)
    q_sum = project(q_sum, 1, 80, 80, left)
    q_sum = project(q_sum, 2, 0, 80, right)
    pieces = ((0, 80, 48), (48, 128, 32))
    for pair, (a, b, n) in zip(forwards, pieces):
        for copy, start in zip(pair, (a, b)):
            copy.wait_recv()
            q_sum = project(q_sum, 3, start, n, far)
            if n == 48:
                grad_add(3, start, n, far)

    def to_block(slots, me, count, where):
        copies = [send(slots.at[me], slots.at[me], peer) for peer in where]
        if count == 4:
            grad_add(3, 48, 32, far) if slots is qy else grad_add(3, 128, 32, far)
        for copy in copies:
            copy.wait_recv()
        total = slots[0]
        for i in range(1, count):
            total = total + slots[i]
        return total

    for w in range(2):
        qc[c, w * 32 : (w + 1) * 32, :] = q_sum[w]
    qy[yi] = to_block(qc, c, 2, [other_core])
    qx[xi] = to_block(qy, yi, 4, y_peer[1:])
    qz[zl] = to_block(qx, xi, 4, x_peer[1:])
    q_all = to_block(qz, zl, 2, [other_zl])
    for w in range(2):
        q_out[w] = q_all[w * 32 : (w + 1) * 32]

    scaled = q_all * (1.0 / 64.0)
    q_hi = scaled.astype(BF16)
    q_low = (scaled - q_hi.astype(F32)).astype(BF16)
    none = jnp.zeros((32, 128), BF16)

    def spread(m):
        return jnp.concatenate(
            [jnp.concatenate([m[:32], none], axis=1), jnp.concatenate([none, m[32:]], axis=1)], axis=0
        )

    right1 = jnp.concatenate([spread(q_hi), spread(q_hi)], axis=0)
    right2 = jnp.concatenate([spread(q_low), jnp.zeros((64, 256), BF16)], axis=0)

    def store(i):
        at = tile_at(i)
        return pltpu.make_async_copy(ev.at[:, at], ne_ref.at[:, at], out_sem.at[i])

    def last_tile(i, carry):
        at = tile_at(i)
        b = bt[at, :]
        update = nn(b, right1) + nn(b, right2)
        for w in range(2):
            cols = slice(w * 128, (w + 1) * 128)
            merged = g[at, cols] + ev[w, at, :].astype(F32)
            ev[w, at, :] = (merged - update[:, cols]).astype(BF16)
        store(i).start()
        return carry

    lax.fori_loop(0, D // TILE, last_tile, 0)

    def wait_tile(i, carry):
        store(i).wait()
        return carry

    lax.fori_loop(0, D // TILE, wait_tile, 0)
    for copy in started:
        if copy is not step6:
            copy.wait_send()


N_COPIES = 64


def local(inputs, kv_grads, error, q_init):
    vmem = pl.BlockSpec(memory_space=pltpu.VMEM)
    anywhere = pl.BlockSpec(memory_space=pl.ANY)
    p_t, q_t, new_error = pl.pallas_call(
        kernel,
        out_shape=(
            jax.ShapeDtypeStruct((2, 32, 128), F32),
            jax.ShapeDtypeStruct((2, 32, 128), F32),
            jax.ShapeDtypeStruct((2, D, 128), BF16),
        ),
        in_specs=[anywhere, vmem, anywhere, vmem],
        out_specs=(vmem, vmem, anywhere),
        scratch_shapes=[
            pltpu.VMEM((4, TOK, D), BF16),
            pltpu.VMEM((640, 256), BF16),
            pltpu.VMEM((4, 64, 256), F32),
            pltpu.VMEM((4, 64, 256), F32),
            pltpu.VMEM((768, TOK), BF16),
            pltpu.VMEM((256, HALF), F32),
            pltpu.VMEM((256, HALF), F32),
            pltpu.VMEM((256, HALF), F32),
            pltpu.VMEM((3, 256, TILE), F32),
            pltpu.VMEM((3, 256, TILE), F32),
            pltpu.VMEM((256, TILE), F32),
            pltpu.VMEM((256, TILE), F32),
            pltpu.VMEM((3, 256, 128), F32),
            pltpu.VMEM((3, 256, 128), F32),
            pltpu.VMEM((2, 256, 128), F32),
            pltpu.VMEM((7, 64, 128), F32),
            pltpu.VMEM((2, 64, 128), F32),
            pltpu.VMEM((64, TILE), F32),
            pltpu.VMEM((64, TILE), F32),
            pltpu.VMEM((64, D), F32),
            pltpu.VMEM((192, D), BF16),
            pltpu.VMEM((D, 128), BF16),
            pltpu.VMEM((2, D, 128), BF16),
            pltpu.VMEM((D, 256), F32),
            pltpu.VMEM((2, 64, 128), F32),
            pltpu.VMEM((4, 64, 128), F32),
            pltpu.VMEM((4, 64, 128), F32),
            pltpu.VMEM((2, 64, 128), F32),
            pltpu.SemaphoreType.DMA((N_COPIES,)),
            pltpu.SemaphoreType.DMA((N_COPIES,)),
            pltpu.SemaphoreType.DMA((2,)),
            pltpu.SemaphoreType.DMA((D // TILE,)),
        ],
        compiler_params=pltpu.CompilerParams(
            collective_id=0, has_side_effects=True, vmem_limit_bytes=60 * 1024 * 1024
        ),
    )(inputs, kv_grads, error[:, 0], jnp.swapaxes(q_init, 1, 2))
    return (jnp.swapaxes(p_t, 1, 2), jnp.swapaxes(q_t, 1, 2), new_error[:, None])


def solution(mesh):
    in_specs = (
        P(("dp", "tensor"), None),
        P(None, "dp", "tensor"),
        P(None, "dp", None, "tensor"),
        P(None, "tensor", None),
    )
    out_specs = (P(None, "dp", "tensor"), P(None, "tensor", None), P(None, "dp", None, "tensor"))
    return jax.shard_map(local, mesh=mesh, in_specs=in_specs, out_specs=out_specs, check_vma=False)
```

time: 1430 us -> 256 us (0.18)
  waiting for transfers between devices: 744 us -> 0 us
  blocking collectives: 275 us -> 0 us
  Pallas kernels: 0 us -> 247 us
  matrix products: 198 us -> 0 us
  local copies, waits for them, and re-layouts: 114 us -> 7.22 us
  other arithmetic: 79.5 us -> 0 us
    psum x1 -> x0, waiting for transfers between devices: 556 us -> none  [local(): summed_factor = lax.psum(factor, 'dp')]
    psum x1 -> x0, blocking collectives: 275 us -> none  [local(): q_factor = lax.psum(projected, 'dp')]
    pallas_call x0 -> x1, Pallas kernels: none -> 247 us  [local(): pl.pallas_call(kernel, out_shape=(jax.ShapeDtypeStruct((2, 32, 128), F32)...]
    dot_general x68 -> x0, matrix products: 198 us -> none  [the longest x32 90.8 us: add_column(): coeffs = jnp.dot(columns_done.T, vector, precision=lax.Precision.HIGHEST)]
    all_gather x1 -> x0, waiting for transfers between devices: 188 us -> none  [local(): lax.all_gather(inputs, 'tensor', axis=0, tiled=True)]
    gather x32 -> x0, local copies, waits for them, and re-layouts: 55.6 us -> none  [add_column(): vector = lax.dynamic_slice_in_dim(matrix, position, 1, 1)]
    scatter x32 -> x0, other arithmetic: 45.3 us -> none  [add_column(): return lax.dynamic_update_slice_in_dim(columns_done, vector, position, 1)]
    another operation x32 -> x0, other arithmetic: 23 us -> none
  transfers between devices with their start and end apart: 2 -> 0, of which waited for: 2 -> 0; matrix products, arithmetic and copies ran while one was open for 0% -> 0% of each run, Pallas kernels for 0% -> 0%
where the time goes in v1:
time: 256 us; the launch traced here: 255 us
  Pallas kernels  247 us (96%)
  local copies, waits for them, and re-layouts  7.22 us (3%)
    pallas_call x1, Pallas kernels, local(): pl.pallas_call(kernel, out_shape=(jax.ShapeDtypeStruct((2, 32, 128), F32)...  247 us
    unnamed x3, local copies, waits for them, and re-layouts  7.22 us

profile of v1, /device:TPU:1, one launch (start us, length us, event | category | flops | bytes accessed | tf_op | source)
XLA Modules:
  0.0 255.0 jit_solution(18044563953921641590)
XLA Ops:
  0.6 247.1 %shard_map.67 = (f32[2,32,128]{2,1,0:T(8,128)}, f32[2,32,128]{2,1,0:T(8,128)}, bf16[2,8192,128]{2,1,0:T(8,128)(2,1)}) custom-call(bf16[160,8192]{1,0:T(8,128)(2,1)} %x_ref.1, bf16[2,640,128]{2,1,0:T(8,128)(2,1)} %k_ref.1, bf16[2,8192,128]{2,1,0:T(8,128)(2,1)} %bitcast.7, f32[2,32,128]{2,1,0:T(8,128)} %bitcast.9), custom_call_target="tpu_custom_call" | custom-call | tf_op jit(solution)/shard_map/pallas_call | solution.py:433
  247.7 1.4 copy.11
  249.1 1.4 copy.12
  250.5 4.5 %copy.13 = bf16[2,1,8192,128]{3,2,1,0:T(8,128)(2,1)} copy(bf16[2,1,8192,128]{3,2,1,0:T(8,128)(2,1)} %bitcast.8) | data formatting | bytes 8388608

commit v2 on v1

v2 whole, which is shorter than its diff:
```python
import functools

import jax
import jax.numpy as jnp
from jax import lax
from jax.experimental import pallas as pl
from jax.experimental.pallas import tpu as pltpu
from jax.sharding import PartitionSpec as P

MESH = pl.DeviceIdType.MESH
F32 = jnp.float32
BF16 = jnp.bfloat16

D = 8192
HALF = D // 2
TOK = 160
TILE = 512


def nt(a, b):
    return lax.dot_general(a, b, (((1,), (1,)), ((), ())), preferred_element_type=F32)


def tn(a, b):
    return lax.dot_general(a, b, (((0,), (0,)), ((), ())), preferred_element_type=F32)


def nn(a, b):
    return jnp.dot(a, b, preferred_element_type=F32)


def parts3(a):
    hi = a.astype(BF16)
    rest = a - hi.astype(F32)
    mid = rest.astype(BF16)
    low = (rest - mid.astype(F32)).astype(BF16)
    return hi, mid, low


def stacked3(a):
    return jnp.concatenate(parts3(a), axis=0)


def sum3(r):
    n = r.shape[0] // 3
    return (r[2 * n :] + r[n : 2 * n]) + r[:n]


def whitener(gram):
    rows = lax.broadcasted_iota(jnp.int32, (2, 32, 64), 1)
    cols = lax.broadcasted_iota(jnp.int32, (2, 32, 64), 2)
    eye = jnp.where(
        lax.broadcasted_iota(jnp.int32, (32, 32), 0) == lax.broadcasted_iota(jnp.int32, (32, 32), 1), 1.0, 0.0
    ).astype(F32)
    a = jnp.stack(
        [
            jnp.concatenate([gram[:32, :32], eye], axis=1),
            jnp.concatenate([gram[32:, 32:], eye], axis=1),
        ]
    )
    for j in range(31):
        scale = a[:, :, j : j + 1] / a[:, j : j + 1, j : j + 1]
        a = a - jnp.where(rows > j, scale * a[:, j : j + 1, :], 0.0)
    pivots = jnp.sum(jnp.where(rows == cols, a, 0.0), axis=2, keepdims=True)
    w = a[:, :, 32:] * (1.0 / jnp.sqrt(pivots))
    zero = jnp.zeros((32, 32), F32)
    return jnp.concatenate(
        [jnp.concatenate([w[0], zero], axis=1), jnp.concatenate([zero, w[1]], axis=1)], axis=0
    )


def diagonal(m):
    none = jnp.zeros((32, m.shape[1]), m.dtype)
    return jnp.concatenate(
        [jnp.concatenate([m[:32], none], axis=1), jnp.concatenate([none, m[32:]], axis=1)], axis=0
    )


def blocks(m):
    n = m.shape[1] // 2
    return jnp.concatenate([m[:32, :n], m[32:, n:]], axis=0)


def kernel(
    x_ref, k_ref, e_ref, q_ref, p_out, q_out, ne_ref,
    xs, k2, qv, ks, kr, kl, fo, fp, rc, ra, rb, a1, b1, ra2, rb2, ab, rz, fab, ga, gb, ft, b2, bt, ev, g,
    qa, qb, send_sem, recv_sem, local_sem, out_sem,
):
    t = lax.axis_index("tensor")
    dp = lax.axis_index("dp")
    c = lax.rem(dp, 2)
    yi = lax.rem(lax.div(dp, 2), 4)
    xi = lax.rem(lax.div(dp, 8), 4)
    zl = lax.div(dp, 32)
    zi = 2 * t + zl

    def device(x=xi, y=yi, z=zi, core=c):
        return {"dp": lax.rem(z, 2) * 32 + x * 8 + y * 2 + core, "tensor": lax.div(z, 2)}

    other_core = device(core=1 - c)
    other_zl = device(z=2 * t + 1 - zl)
    x_peer = [None] + [device(x=lax.rem(xi + o, 4)) for o in (1, 2, 3)]
    y_peer = [None] + [device(y=lax.rem(yi + o, 4)) for o in (1, 2, 3)]
    z_peer = [None] + [device(z=lax.rem(zi + o, 8)) for o in range(1, 8)]
    y_core_peer = [device(y=lax.rem(yi + o, 4), core=1 - c) for o in (1, 2, 3)]
    x_zl_peer = [device(x=lax.rem(xi + o, 4), z=2 * t + 1 - zl) for o in (1, 2, 3)]
    t_right, t_left = z_peer[2], z_peer[6]

    barrier = pltpu.get_barrier_semaphore()
    peers = [other_core] + x_peer[1:] + y_peer[1:] + z_peer[1:] + y_core_peer + x_zl_peer
    for peer in peers:
        pl.semaphore_signal(barrier, inc=1, device_id=peer, device_id_type=MESH)

    started = []

    def send(src, dst, where):
        i = len(started)
        copy = pltpu.make_async_remote_copy(
            src_ref=src, dst_ref=dst, send_sem=send_sem.at[i], recv_sem=recv_sem.at[i],
            device_id=where, device_id_type=MESH,
        )
        copy.start()
        started.append(copy)
        return copy

    def load(src, dst, i):
        copy = pltpu.make_async_copy(src, dst, local_sem.at[i])
        copy.start()
        return copy

    def tile_at(i):
        return pl.ds(pl.multiple_of(i * TILE, TILE), TILE)

    owners = [t, lax.rem(t + 3, 4), lax.rem(t + 1, 4), lax.rem(t + 2, 4)]
    loads = [load(q_ref, qv, 0)]
    for slot in range(4):
        there = pl.ds(pl.multiple_of(owners[slot] * TOK, 16), TOK)
        for w in range(2):
            here = k2.at[pl.ds(slot * TOK, TOK), pl.ds(w * 128, 128)]
            loads.append(load(k_ref.at[w, there], here, 1 + 2 * slot + w))
    load_x = load(x_ref, xs.at[pl.ds(0, TOK)], 9)
    load_e = [load(e_ref.at[w], ev.at[:, pl.ds(w * 128, 128)], 10 + w) for w in range(2)]

    pl.semaphore_wait(barrier, len(peers))

    def rows(start, size):
        return xs.at[pl.ds(start, size)]

    def token_pair(to_right, to_left, size):
        return (
            send(x_ref.at[pl.ds(to_right, size)], rows(TOK + to_right, size), t_right),
            send(x_ref.at[pl.ds(to_left, size)], rows(2 * TOK + to_left, size), t_left),
        )

    first = token_pair(0, 80, 16)

    for copy in loads:
        copy.wait()
    none = jnp.zeros((32, 128), F32)
    q3 = stacked3(
        jnp.concatenate(
            [jnp.concatenate([qv[0], none], axis=1), jnp.concatenate([none, qv[1]], axis=1)], axis=0
        )
    )
    kq = []
    for slot, o in ((3, 4), (1, 6), (2, 2), (0, 0)):
        r = sum3(nt(q3, k2[slot * TOK : (slot + 1) * TOK, :]))
        ref = ks.at[slot] if o else kr.at[t]
        ref[0:64, :] = r[:, 0:128]
        for i in range(4):
            ref[64:80, 32 * i : 32 * i + 32] = r[16 * i : 16 * i + 16, 128:TOK]
        if o:
            kq.append(send(ks.at[slot], kr.at[t], z_peer[o]))

    first = first + token_pair(16, 96, 64)

    load_x.wait()
    for copy in load_e:
        copy.wait()
    for copy in kq:
        copy.wait_recv()
    for s in range(4):
        for i, part in enumerate(parts3(kr[s, 0:64, :])):
            kl[i * 256 + s * 64 : i * 256 + s * 64 + 64, 0:128] = part
        for i, part in enumerate(parts3(kr[s, 64:80, :])):
            for j in range(4):
                at = i * 256 + s * 64 + j * 16
                kl[at : at + 16, 128:TOK] = part[:, 32 * j : 32 * j + 32]
    mine = pl.ds(pl.multiple_of(t * 64, 64), 64)

    def factor_tile(ref, at, there):
        at = pl.ds(at, TILE)
        ref[:, at] = sum3(nn(kl[...], xs[0:TOK, pl.ds(there, TILE)]))
        ref[mine, at] += sum3(nt(q3, ev[pl.ds(there, TILE), :]))

    core_copies = []
    for piece in range(2):

        def partner_tile(i, carry, piece=piece):
            at = pl.multiple_of(piece * 2048 + i * TILE, TILE)
            factor_tile(fp, at, pl.multiple_of((1 - c) * HALF + at, TILE))
            return carry

        lax.fori_loop(0, 4, partner_tile, 0, unroll=2)
        part = pl.ds(piece * 2048, 2048)
        core_copies.append(send(fp.at[:, part], rc.at[:, part], other_core))

    def own_tile(i, carry):
        at = pl.multiple_of(i * TILE, TILE)
        factor_tile(fo, at, pl.multiple_of(c * HALF + at, TILE))
        return carry

    lax.fori_loop(0, 8, own_tile, 0, unroll=2)

    for copy in core_copies:
        copy.wait_recv()

    def add_core(start):
        def some_rows(i, carry):
            r = pl.ds(pl.multiple_of(i * 32, 32), 32)
            fo[r, pl.ds(start, TILE)] += rc[r, pl.ds(start, TILE)]
            return carry

        lax.fori_loop(0, 8, some_rows, 0)

    step1 = []
    for o in (2, 1, 3, 0):
        at_x = pl.multiple_of(lax.rem(xi + o, 4) * TILE, TILE)
        at_y = pl.multiple_of(2048 + lax.rem(yi + o, 4) * TILE, TILE)
        add_core(at_x)
        if o:
            step1.append(send(fo.at[:, pl.ds(at_x, TILE)], ra.at[o - 1], x_peer[o]))
        add_core(at_y)
        if o:
            step1.append(send(fo.at[:, pl.ds(at_y, TILE)], rb.at[o - 1], y_peer[o]))
    for copy in step1:
        copy.wait_recv()

    at_x = pl.multiple_of(xi * TILE, TILE)
    at_y = pl.multiple_of(2048 + yi * TILE, TILE)

    def sum_step1(i, carry):
        r = pl.ds(pl.multiple_of(i * 32, 32), 32)
        a1[r, :] = ((fo[r, pl.ds(at_x, TILE)] + ra[0, r, :]) + ra[1, r, :]) + ra[2, r, :]
        b1[r, :] = ((fo[r, pl.ds(at_y, TILE)] + rb[0, r, :]) + rb[1, r, :]) + rb[2, r, :]
        return carry

    lax.fori_loop(0, 8, sum_step1, 0)

    step2 = []
    for o in (2, 1, 3):
        to_y = pl.ds(pl.multiple_of(lax.rem(yi + o, 4) * 128, 128), 128)
        to_x = pl.ds(pl.multiple_of(lax.rem(xi + o, 4) * 128, 128), 128)
        step2.append(send(a1.at[:, to_y], ra2.at[o - 1], y_peer[o]))
        step2.append(send(b1.at[:, to_x], rb2.at[o - 1], x_peer[o]))
    for copy in step2:
        copy.wait_recv()
    at_y = pl.ds(pl.multiple_of(yi * 128, 128), 128)
    at_x = pl.ds(pl.multiple_of(xi * 128, 128), 128)
    ab[0] = ((a1[:, at_y] + ra2[0]) + ra2[1]) + ra2[2]
    ab[1] = ((b1[:, at_x] + rb2[0]) + rb2[1]) + rb2[2]

    step3 = []
    for o in (4, 3, 5, 2, 6, 1, 7):
        z = lax.rem(zi + o, 8)
        there = pl.ds(pl.multiple_of(lax.div(z, 2) * 64, 64), 64)
        step3.append(send(ab.at[lax.rem(z, 2), there], rz.at[o - 1], z_peer[o]))
    second = token_pair(80, 48, 32)
    for copy in step3:
        copy.wait_recv()
    total = ab[zl, mine, :]
    for o in range(7):
        total = total + rz[o]
    fab[zl] = total
    zl_copy = send(fab.at[zl], fab.at[zl], other_zl)
    third = token_pair(112, 0, 48)

    for copy in first:
        copy.wait_recv()
    forwards = [
        (send(rows(160, 64), rows(480, 64), t_right), send(rows(416, 64), rows(576, 64), t_left)),
        (send(rows(224, 16), rows(544, 16), t_right), send(rows(400, 16), rows(560, 16), t_left)),
    ]

    def grad_pass(start, size, mode):
        k = k2[start : start + size, :]

        def tile(i, carry):
            at = tile_at(i)
            more = tn(xs[start : start + size, at], k)
            if mode == "first":
                g[at, :] = more + ev[at, :].astype(F32)
            else:
                g[at, :] += more
            return carry

        lax.fori_loop(0, D // TILE, tile, 0, unroll=4)

    grad_pass(0, 240, "first")

    zl_copy.wait_recv()
    step4 = []
    for o in (2, 1, 3):
        step4.append(send(fab.at[0], ga.at[:, at_y], y_peer[o]))
        step4.append(send(fab.at[1], gb.at[:, at_x], x_peer[o]))
    ga[:, at_y] = fab[0]
    gb[:, at_x] = fab[1]
    for copy in step4:
        copy.wait_recv()
    own_a = pl.ds(pl.multiple_of(c * HALF + xi * TILE, TILE), TILE)
    own_b = pl.ds(pl.multiple_of(c * HALF + 2048 + yi * TILE, TILE), TILE)
    step5 = []
    for o in (2, 1, 3):
        step5.append(send(ga, ft.at[:, own_a], x_peer[o]))
        step5.append(send(gb, ft.at[:, own_b], y_peer[o]))
    ft[:, own_a] = ga[...]
    ft[:, own_b] = gb[...]
    for copy in step5:
        copy.wait_recv()
    own_half = pl.ds(pl.multiple_of(c * HALF, HALF), HALF)
    step6 = send(ft.at[:, own_half], ft.at[:, own_half], other_core)
    step6.wait()

    def gram_of(acc):
        rows3 = acc[0:64] + acc[64:128] + acc[128:192]
        return rows3[:, 0:64] + rows3[:, 64:128] + rows3[:, 128:192]

    def thrice(w):
        return jnp.concatenate([jnp.concatenate([p, p, p], axis=1) for p in parts3(w)], axis=0)

    def gram_tile(i, acc):
        f = stacked3(ft[:, tile_at(i)])
        return acc + nt(f, f)

    none = jnp.zeros((192, 192), F32)
    w1 = thrice(whitener(gram_of(lax.fori_loop(0, D // TILE, gram_tile, none, unroll=4))))

    def first_round(i, acc):
        b = sum3(nn(w1, stacked3(ft[:, tile_at(i)])))
        ft[:, tile_at(i)] = b
        b = stacked3(b)
        return acc + nt(b, b)

    w2 = thrice(whitener(gram_of(lax.fori_loop(0, D // TILE, first_round, none, unroll=4))))

    def second_round(i, carry):
        b = sum3(nn(w2, stacked3(ft[:, tile_at(i)])))
        ft[:, tile_at(i)] = b
        hi = b.astype(BF16)
        rest = b - hi.astype(F32)
        b2[0:64, tile_at(i)] = hi
        b2[64:128, tile_at(i)] = rest.astype(BF16)
        flipped = jnp.concatenate([b, rest], axis=0).T.astype(BF16)
        bt[tile_at(i), 0:128] = flipped
        bt[tile_at(i), 128:256] = flipped
        return carry

    lax.fori_loop(0, D // TILE, second_round, 0, unroll=4)
    own_rows = pl.ds(pl.multiple_of(dp * 128, 128), 128)
    for w in range(2):
        p_out[w] = ft[w * 32 : (w + 1) * 32, own_rows]

    def error_tile(i, acc):
        return acc + nn(b2[:, tile_at(i)], ev[tile_at(i), :])

    by_w = lax.fori_loop(0, D // TILE, error_tile, jnp.zeros((128, 256), F32), unroll=4)
    q_sum = blocks(by_w[64:] + by_w[:64])

    def project(start, size):
        def tile(i, acc):
            return acc + nt(b2[:, tile_at(i)], xs[start : start + size, tile_at(i)])

        z = lax.fori_loop(0, D // TILE, tile, jnp.zeros((128, size), F32), unroll=4)
        z = stacked3(z[64:] + z[:64])
        return blocks(sum3(nn(z, k2[start : start + size, :])))

    q_sum = q_sum + project(0, 240)
    for copy in second + third:
        copy.wait_recv()
    grad_pass(240, 240, "more")
    q_sum = q_sum + project(240, 240)
    for copy, start in zip(forwards[0], (480, 576)):
        copy.wait_recv()
        q_sum = q_sum + project(start, 64)
    for copy in forwards[1]:
        copy.wait_recv()
    q_sum = q_sum + project(544, 32)

    def sum_of(slots, me, where, meanwhile):
        copies = [send(slots.at[me], slots.at[me], peer) for peer in where]
        meanwhile()
        for copy in copies:
            copy.wait_recv()
        total = slots[0]
        for i in range(1, 8):
            total = total + slots[i]
        return total

    qa[yi * 2 + c] = q_sum
    qb[xi * 2 + zl] = sum_of(
        qa, yi * 2 + c, y_peer[1:] + y_core_peer + [other_core], lambda: grad_pass(480, 160, "more")
    )
    q_all = sum_of(qb, xi * 2 + zl, x_peer[1:] + x_zl_peer + [other_zl], lambda: None)
    for w in range(2):
        q_out[w] = q_all[w * 32 : (w + 1) * 32]

    scaled = q_all * (1.0 / 64.0)
    q_hi = diagonal(scaled.astype(BF16))
    q_low = diagonal((scaled - scaled.astype(BF16).astype(F32)).astype(BF16))
    q_parts = jnp.concatenate([q_hi, q_hi, q_low, jnp.zeros((64, 256), BF16)], axis=0)

    def stores(i):
        return [
            pltpu.make_async_copy(
                ev.at[tile_at(i), pl.ds(w * 128, 128)], ne_ref.at[w, tile_at(i)], out_sem.at[i, w]
            )
            for w in range(2)
        ]

    def last_tile(i, carry):
        at = tile_at(i)
        ev[at, :] = (g[at, :] - nn(bt[at, :], q_parts)).astype(BF16)
        for copy in stores(i):
            copy.start()
        return carry

    lax.fori_loop(0, D // TILE, last_tile, 0, unroll=2)

    def wait_tile(i, carry):
        for copy in stores(i):
            copy.wait()
        return carry

    lax.fori_loop(0, D // TILE, wait_tile, 0)
    for copy in started:
        if copy is not step6:
            copy.wait_send()


N_PIECES = 8


def hand_on(p_ref, q_ref, ne_ref, p_out, q_out, ne_out, held, in_sem, out_sem):
    size = D // N_PIECES
    pieces = [(w, pl.ds(i * size, size)) for i in range(N_PIECES) for w in range(2)]
    loads = [pltpu.make_async_copy(ne_ref.at[at], held.at[at], in_sem.at[i]) for i, at in enumerate(pieces)]
    stores = [pltpu.make_async_copy(held.at[at], ne_out.at[at], out_sem.at[i]) for i, at in enumerate(pieces)]
    for copy in loads:
        copy.start()
    p_out[...] = p_ref[...]
    q_out[...] = q_ref[...]
    for there, back in zip(loads, stores):
        there.wait()
        back.start()
    for copy in stores:
        copy.wait()


N_COPIES = 64


def local(inputs, kv_grads, error, q_init):
    vmem = pl.BlockSpec(memory_space=pltpu.VMEM)
    anywhere = pl.BlockSpec(memory_space=pl.ANY)
    shapes = (
        jax.ShapeDtypeStruct((2, 32, 128), F32),
        jax.ShapeDtypeStruct((2, 32, 128), F32),
        jax.ShapeDtypeStruct((2, D, 128), BF16),
    )
    results = pl.pallas_call(
        kernel,
        out_shape=shapes,
        in_specs=[anywhere] * 4,
        out_specs=(vmem, vmem, anywhere),
        scratch_shapes=[
            pltpu.VMEM((4 * TOK, D), BF16),
            pltpu.VMEM((4 * TOK, 256), BF16),
            pltpu.VMEM((2, 32, 128), F32),
            pltpu.VMEM((4, 80, 128), F32),
            pltpu.VMEM((4, 80, 128), F32),
            pltpu.VMEM((768, TOK), BF16),
            pltpu.VMEM((256, HALF), F32),
            pltpu.VMEM((256, HALF), F32),
            pltpu.VMEM((256, HALF), F32),
            pltpu.VMEM((3, 256, TILE), F32),
            pltpu.VMEM((3, 256, TILE), F32),
            pltpu.VMEM((256, TILE), F32),
            pltpu.VMEM((256, TILE), F32),
            pltpu.VMEM((3, 256, 128), F32),
            pltpu.VMEM((3, 256, 128), F32),
            pltpu.VMEM((2, 256, 128), F32),
            pltpu.VMEM((7, 64, 128), F32),
            pltpu.VMEM((2, 64, 128), F32),
            pltpu.VMEM((64, TILE), F32),
            pltpu.VMEM((64, TILE), F32),
            pltpu.VMEM((64, D), F32),
            pltpu.VMEM((128, D), BF16),
            pltpu.VMEM((D, 256), BF16),
            pltpu.VMEM((D, 256), BF16),
            pltpu.VMEM((D, 256), F32),
            pltpu.VMEM((8, 64, 128), F32),
            pltpu.VMEM((8, 64, 128), F32),
            pltpu.SemaphoreType.DMA((N_COPIES,)),
            pltpu.SemaphoreType.DMA((N_COPIES,)),
            pltpu.SemaphoreType.DMA((12,)),
            pltpu.SemaphoreType.DMA((D // TILE, 2)),
        ],
        compiler_params=pltpu.CompilerParams(
            collective_id=0, has_side_effects=True, vmem_limit_bytes=60 * 1024 * 1024
        ),
    )(inputs, kv_grads, error[:, 0], jnp.swapaxes(q_init, 1, 2))
    p_t, q_t, new_error = pl.pallas_call(
        hand_on,
        out_shape=shapes,
        in_specs=[vmem, vmem, anywhere],
        out_specs=(vmem, vmem, anywhere),
        scratch_shapes=[
            pltpu.VMEM((2, D, 128), BF16),
            pltpu.SemaphoreType.DMA((2 * N_PIECES,)),
            pltpu.SemaphoreType.DMA((2 * N_PIECES,)),
        ],
        compiler_params=pltpu.CompilerParams(vmem_limit_bytes=60 * 1024 * 1024),
    )(*results)
    return (jnp.swapaxes(p_t, 1, 2), jnp.swapaxes(q_t, 1, 2), new_error[:, None])


def solution(mesh):
    in_specs = (
        P(("dp", "tensor"), None),
        P(None, "dp", "tensor"),
        P(None, "dp", None, "tensor"),
        P(None, "tensor", None),
    )
    out_specs = (P(None, "dp", "tensor"), P(None, "tensor", None), P(None, "dp", None, "tensor"))
    return jax.shard_map(local, mesh=mesh, in_specs=in_specs, out_specs=out_specs, check_vma=False)
```

time: 256 us -> 216 us (0.84)
  Pallas kernels: 247 us -> 215 us
  local copies, waits for them, and re-layouts: 7.22 us -> 0 us
    pallas_call x1 -> x2, Pallas kernels: 247 us -> 215 us  [the longest x1 210 us: local(): pl.pallas_call(kernel, out_shape=shapes, in_specs=[anywhere] * 4, out_spe...]
    unnamed x3 -> x0, local copies, waits for them, and re-layouts: 7.22 us -> none
where the time goes in v2:
time: 216 us
  Pallas kernels  215 us (100%)
    pallas_call x1, Pallas kernels, local(): pl.pallas_call(kernel, out_shape=shapes, in_specs=[anywhere] * 4, out_spe...  210 us
    pallas_call x1, Pallas kernels, local(): pl.pallas_call(hand_on, out_shape=shapes, in_specs=[vmem, vmem, anywhere]...  5.25 us

profile of v2, /device:TPU:1, one launch (start us, length us, event | category | flops | bytes accessed | tf_op | source)
XLA Modules:
  0.0 215.8 jit_solution(6648668774901477054)
XLA Ops:
  0.6 209.9 %shard_map.67 = (f32[2,32,128]{2,1,0:T(8,128)}, f32[2,32,128]{2,1,0:T(8,128)}, bf16[2,8192,128]{2,1,0:T(8,128)(2,1)}) custom-call(bf16[160,8192]{1,0:T(8,128)(2,1)} %x_ref.1, bf16[2,640,128]{2,1,0:T(8,128)(2,1)} %k_ref.1, bf16[2,8192,128]{2,1,0:T(8,128)(2,1)} %bitcast.7, f32[2,32,128]{2,1,0:T(8,128)} %bitcast.8), custom_call_target="tpu_custom_call" | custom-call | tf_op jit(solution)/shard_map/pallas_call | solution.py:470
  210.5 5.3 %shard_map.68 = (f32[2,32,128]{2,1,0:T(8,128)}, f32[2,32,128]{2,1,0:T(8,128)}, bf16[2,8192,128]{2,1,0:T(8,128)(2,1)}) custom-call(f32[2,32,128]{2,1,0:T(8,128)} %get-tuple-element.9.p_ref, f32[2,32,128]{2,1,0:T(8,128)} %get-tuple-element.10.q_ref, bf16[2,8192,128]{2,1,0:T(8,128)(2,1)} %get-tuple-element.11.ne_ref), custom_call_target="tpu_custom_call" | custom-call | tf_op jit(solution)/shard_map/pallas_call | solution.py:512

commit v3 on v2

--- a/solution.py
+++ b/solution.py
@@ -82,7 +82,7 @@
 
 
 def kernel(
-    x_ref, k_ref, e_ref, q_ref, p_out, q_out, ne_ref,
+    x_ref, k_ref, e_ref, q_ref, p_out, q_out, merged_out, bt_out,
     xs, k2, qv, ks, kr, kl, fo, fp, rc, ra, rb, a1, b1, ra2, rb2, ab, rz, fab, ga, gb, ft, b2, bt, ev, g,
     qa, qb, send_sem, recv_sem, local_sem, out_sem,
 ):
@@ -292,9 +292,14 @@
                 g[at, :] = more + ev[at, :].astype(F32)
             else:
                 g[at, :] += more
+            if mode == "last":
+                store(i).start()
             return carry
 
         lax.fori_loop(0, D // TILE, tile, 0, unroll=4)
+
+    def store(i):
+        return pltpu.make_async_copy(g.at[tile_at(i)], merged_out.at[tile_at(i)], out_sem.at[i])
 
     grad_pass(0, 240, "first")
 
@@ -350,15 +355,13 @@
         rest = b - hi.astype(F32)
         b2[0:64, tile_at(i)] = hi
         b2[64:128, tile_at(i)] = rest.astype(BF16)
-        flipped = jnp.concatenate([b, rest], axis=0).T.astype(BF16)
-        bt[tile_at(i), 0:128] = flipped
-        bt[tile_at(i), 128:256] = flipped
+        bt[tile_at(i), :] = jnp.concatenate([b, rest], axis=0).T.astype(BF16)
         return carry
 
     lax.fori_loop(0, D // TILE, second_round, 0, unroll=4)
+    store_bt = load(bt, bt_out, 12)
     own_rows = pl.ds(pl.multiple_of(dp * 128, 128), 128)
-    for w in range(2):
-        p_out[w] = ft[w * 32 : (w + 1) * 32, own_rows]
+    store_p = [load(ft.at[pl.ds(w * 32, 32), own_rows], p_out.at[w], 13 + w) for w in range(2)]
 
     def error_tile(i, acc):
         return acc + nn(b2[:, tile_at(i)], ev[tile_at(i), :])
@@ -366,11 +369,11 @@
     by_w = lax.fori_loop(0, D // TILE, error_tile, jnp.zeros((128, 256), F32), unroll=4)
     q_sum = blocks(by_w[64:] + by_w[:64])
 
-    def project(start, size):
+    def project(start, size, unroll=4):
         def tile(i, acc):
             return acc + nt(b2[:, tile_at(i)], xs[start : start + size, tile_at(i)])
 
-        z = lax.fori_loop(0, D // TILE, tile, jnp.zeros((128, size), F32), unroll=4)
+        z = lax.fori_loop(0, D // TILE, tile, jnp.zeros((128, size), F32), unroll=unroll)
         z = stacked3(z[64:] + z[:64])
         return blocks(sum3(nn(z, k2[start : start + size, :])))
 
@@ -379,12 +382,21 @@
         copy.wait_recv()
     grad_pass(240, 240, "more")
     q_sum = q_sum + project(240, 240)
+    last = forwards[0] + forwards[1]
+    for copy in started:
+        if copy is not step6 and not any(copy is other for other in last):
+            copy.wait_send()
     for copy, start in zip(forwards[0], (480, 576)):
         copy.wait_recv()
         q_sum = q_sum + project(start, 64)
     for copy in forwards[1]:
         copy.wait_recv()
-    q_sum = q_sum + project(544, 32)
+    q_sum = q_sum + project(544, 32, 16)
+
+    early = len(started)
+
+    def far_first(six):
+        return [six[i] for i in (4, 1, 3, 5, 0, 2)]
 
     def sum_of(slots, me, where, meanwhile):
         copies = [send(slots.at[me], slots.at[me], peer) for peer in where]
@@ -398,61 +410,75 @@
 
     qa[yi * 2 + c] = q_sum
     qb[xi * 2 + zl] = sum_of(
-        qa, yi * 2 + c, y_peer[1:] + y_core_peer + [other_core], lambda: grad_pass(480, 160, "more")
+        qa, yi * 2 + c, far_first(y_peer[1:] + y_core_peer) + [other_core], lambda: grad_pass(480, 160, "last")
     )
-    q_all = sum_of(qb, xi * 2 + zl, x_peer[1:] + x_zl_peer + [other_zl], lambda: None)
+    q_all = sum_of(qb, xi * 2 + zl, far_first(x_peer[1:] + x_zl_peer) + [other_zl], lambda: None)
     for w in range(2):
-        q_out[w] = q_all[w * 32 : (w + 1) * 32]
-
-    scaled = q_all * (1.0 / 64.0)
+        qv[w] = q_all[w * 32 : (w + 1) * 32]
+    store_q = load(qv, q_out, 15)
+
+    def wait_tile(i, carry):
+        store(i).wait()
+        return carry
+
+    lax.fori_loop(0, D // TILE, wait_tile, 0)
+    for copy in [store_bt, store_q] + store_p:
+        copy.wait()
+    for copy in list(last) + started[early:]:
+        copy.wait_send()
+
+
+TILE2 = 1024
+
+
+def update(p_ref, q_ref, merged_ref, bt_ref, p_out, q_out, ne_out, q, m, b, ne, m_sem, b_sem, out_sem, small_sem):
+    def at(i):
+        return pl.ds(pl.multiple_of(i * TILE2, TILE2), TILE2)
+
+    def loads(i):
+        return [
+            pltpu.make_async_copy(bt_ref.at[at(i)], b.at[at(i)], b_sem.at[i]),
+            pltpu.make_async_copy(merged_ref.at[at(i)], m.at[at(i)], m_sem.at[i]),
+        ]
+
+    def store(i):
+        return pltpu.make_async_copy(ne.at[:, at(i)], ne_out.at[:, at(i)], out_sem.at[i])
+
+    load_q = pltpu.make_async_copy(q_ref, q, small_sem.at[0])
+    load_q.start()
+    for i in range(D // TILE2):
+        for copy in loads(i):
+            copy.start()
+    hand_on = [
+        pltpu.make_async_copy(p_ref, p_out, small_sem.at[1]),
+        pltpu.make_async_copy(q_ref, q_out, small_sem.at[2]),
+    ]
+    for copy in hand_on:
+        copy.start()
+    load_q.wait()
+    scaled = jnp.concatenate([q[0], q[1]], axis=0) * (1.0 / 64.0)
     q_hi = diagonal(scaled.astype(BF16))
     q_low = diagonal((scaled - scaled.astype(BF16).astype(F32)).astype(BF16))
     q_parts = jnp.concatenate([q_hi, q_hi, q_low, jnp.zeros((64, 256), BF16)], axis=0)
 
-    def stores(i):
-        return [
-            pltpu.make_async_copy(
-                ev.at[tile_at(i), pl.ds(w * 128, 128)], ne_ref.at[w, tile_at(i)], out_sem.at[i, w]
-            )
-            for w in range(2)
-        ]
-
-    def last_tile(i, carry):
-        at = tile_at(i)
-        ev[at, :] = (g[at, :] - nn(bt[at, :], q_parts)).astype(BF16)
-        for copy in stores(i):
-            copy.start()
+    def tile(i, carry):
+        for copy in loads(i):
+            copy.wait()
+        twice = jnp.concatenate([b[at(i), :], b[at(i), :]], axis=1)
+        rest = (m[at(i), :] - nn(twice, q_parts)).astype(BF16)
+        for w in range(2):
+            ne[w, at(i), :] = rest[:, w * 128 : (w + 1) * 128]
+        store(i).start()
         return carry
 
-    lax.fori_loop(0, D // TILE, last_tile, 0, unroll=2)
+    lax.fori_loop(0, D // TILE2, tile, 0)
 
     def wait_tile(i, carry):
-        for copy in stores(i):
-            copy.wait()
+        store(i).wait()
         return carry
 
-    lax.fori_loop(0, D // TILE, wait_tile, 0)
-    for copy in started:
-        if copy is not step6:
-            copy.wait_send()
-
-
-N_PIECES = 8
-
-
-def hand_on(p_ref, q_ref, ne_ref, p_out, q_out, ne_out, held, in_sem, out_sem):
-    size = D // N_PIECES
-    pieces = [(w, pl.ds(i * size, size)) for i in range(N_PIECES) for w in range(2)]
-    loads = [pltpu.make_async_copy(ne_ref.at[at], held.at[at], in_sem.at[i]) for i, at in enumerate(pieces)]
-    stores = [pltpu.make_async_copy(held.at[at], ne_out.at[at], out_sem.at[i]) for i, at in enumerate(pieces)]
-    for copy in loads:
-        copy.start()
-    p_out[...] = p_ref[...]
-    q_out[...] = q_ref[...]
-    for there, back in zip(loads, stores):
-        there.wait()
-        back.start()
-    for copy in stores:
+    lax.fori_loop(0, D // TILE2, wait_tile, 0)
+    for copy in hand_on:
         copy.wait()
 
 
@@ -460,18 +486,13 @@
 
 
 def local(inputs, kv_grads, error, q_init):
-    vmem = pl.BlockSpec(memory_space=pltpu.VMEM)
     anywhere = pl.BlockSpec(memory_space=pl.ANY)
-    shapes = (
-        jax.ShapeDtypeStruct((2, 32, 128), F32),
-        jax.ShapeDtypeStruct((2, 32, 128), F32),
-        jax.ShapeDtypeStruct((2, D, 128), BF16),
-    )
+    small = jax.ShapeDtypeStruct((2, 32, 128), F32)
     results = pl.pallas_call(
         kernel,
-        out_shape=shapes,
+        out_shape=(small, small, jax.ShapeDtypeStruct((D, 256), F32), jax.ShapeDtypeStruct((D, 128), BF16)),
         in_specs=[anywhere] * 4,
-        out_specs=(vmem, vmem, anywhere),
+        out_specs=(anywhere,) * 4,
         scratch_shapes=[
             pltpu.VMEM((4 * TOK, D), BF16),
             pltpu.VMEM((4 * TOK, 256), BF16),
@@ -495,29 +516,34 @@
             pltpu.VMEM((64, TILE), F32),
             pltpu.VMEM((64, D), F32),
             pltpu.VMEM((128, D), BF16),
-            pltpu.VMEM((D, 256), BF16),
+            pltpu.VMEM((D, 128), BF16),
             pltpu.VMEM((D, 256), BF16),
             pltpu.VMEM((D, 256), F32),
             pltpu.VMEM((8, 64, 128), F32),
             pltpu.VMEM((8, 64, 128), F32),
             pltpu.SemaphoreType.DMA((N_COPIES,)),
             pltpu.SemaphoreType.DMA((N_COPIES,)),
-            pltpu.SemaphoreType.DMA((12,)),
-            pltpu.SemaphoreType.DMA((D // TILE, 2)),
+            pltpu.SemaphoreType.DMA((16,)),
+            pltpu.SemaphoreType.DMA((D // TILE,)),
         ],
         compiler_params=pltpu.CompilerParams(
             collective_id=0, has_side_effects=True, vmem_limit_bytes=60 * 1024 * 1024
         ),
     )(inputs, kv_grads, error[:, 0], jnp.swapaxes(q_init, 1, 2))
     p_t, q_t, new_error = pl.pallas_call(
-        hand_on,
-        out_shape=shapes,
-        in_specs=[vmem, vmem, anywhere],
-        out_specs=(vmem, vmem, anywhere),
+        update,
+        out_shape=(small, small, jax.ShapeDtypeStruct((2, D, 128), BF16)),
+        in_specs=[anywhere] * 4,
+        out_specs=(anywhere,) * 3,
         scratch_shapes=[
+            pltpu.VMEM((2, 32, 128), F32),
+            pltpu.VMEM((D, 256), F32),
+            pltpu.VMEM((D, 128), BF16),
             pltpu.VMEM((2, D, 128), BF16),
-            pltpu.SemaphoreType.DMA((2 * N_PIECES,)),
-            pltpu.SemaphoreType.DMA((2 * N_PIECES,)),
+            pltpu.SemaphoreType.DMA((D // TILE,)),
+            pltpu.SemaphoreType.DMA((D // TILE,)),
+            pltpu.SemaphoreType.DMA((D // TILE,)),
+            pltpu.SemaphoreType.DMA((3,)),
         ],
         compiler_params=pltpu.CompilerParams(vmem_limit_bytes=60 * 1024 * 1024),
     )(*results)

time: 216 us -> 213 us (0.986)
  Pallas kernels: 215 us -> 212 us
    pallas_call x2, Pallas kernels: 215 us -> 212 us  [the longest x1 205 us: local(): pl.pallas_call(kernel, out_shape=(small, small, jax.ShapeDtypeStruct((D,...]
where the time goes in v3:
time: 213 us
  Pallas kernels  212 us (100%)
    pallas_call x1, Pallas kernels, local(): pl.pallas_call(kernel, out_shape=(small, small, jax.ShapeDtypeStruct((D,...  205 us
    pallas_call x1, Pallas kernels, local(): pl.pallas_call(update, out_shape=(small, small, jax.ShapeDtypeStruct((2,...  7.13 us

profile of v3, /device:TPU:1, one launch (start us, length us, event | category | flops | bytes accessed | tf_op | source)
XLA Modules:
  0.0 213.1 jit_solution(1385565626820901924)
XLA Ops:
  0.6 205.3 %shard_map.67 = (f32[2,32,128]{2,1,0:T(8,128)}, f32[2,32,128]{2,1,0:T(8,128)}, f32[8192,256]{1,0:T(8,128)}, bf16[8192,128]{1,0:T(8,128)(2,1)}) custom-call(bf16[160,8192]{1,0:T(8,128)(2,1)} %x_ref.1, bf16[2,640,128]{2,1,0:T(8,128)(2,1)} %k_ref.1, bf16[2,8192,128]{2,1,0:T(8,128)(2,1)} %bitcast.7, f32[2,32,128]{2,1,0:T(8,128)} %bitcast.8), custom_call_target="tpu_custom_call" | custom-call | tf_op jit(solution)/shard_map/pallas_call | solution.py:491
  205.9 7.1 %shard_map.68 = (f32[2,32,128]{2,1,0:T(8,128)}, f32[2,32,128]{2,1,0:T(8,128)}, bf16[2,8192,128]{2,1,0:T(8,128)(2,1)}) custom-call(f32[2,32,128]{2,1,0:T(8,128)} %get-tuple-element.10.p_ref, f32[2,32,128]{2,1,0:T(8,128)} %get-tuple-element.11.q_ref, f32[8192,256]{1,0:T(8,128)} %get-tuple-element.12.merged_ref, bf16[8192,128]{1,0:T(8,128)(2,1)} %get-tuple-element.13.bt_ref), custom_call_target="tpu_custom_call" | custom-call | tf_op jit(solution)/shard_map/pallas_call | solution.py:533

commit v4 on v3

--- a/solution.py
+++ b/solution.py
@@ -428,7 +428,7 @@
         copy.wait_send()
 
 
-TILE2 = 1024
+TILE2 = 2048
 
 
 def update(p_ref, q_ref, merged_ref, bt_ref, p_out, q_out, ne_out, q, m, b, ne, m_sem, b_sem, out_sem, small_sem):

time: 213 us -> 212 us (level)
  no operation moved by 1% of the time
where the time goes in v4:
time: 212 us
  Pallas kernels  212 us (100%)
    pallas_call x1, Pallas kernels, local(): pl.pallas_call(kernel, out_shape=(small, small, jax.ShapeDtypeStruct((D,...  205 us
    pallas_call x1, Pallas kernels, local(): pl.pallas_call(update, out_shape=(small, small, jax.ShapeDtypeStruct((2,...  6.36 us

profile of v4, /device:TPU:1, one launch (start us, length us, event | category | flops | bytes accessed | tf_op | source)
XLA Modules:
  0.0 212.3 jit_solution(10679924328938881087)
XLA Ops:
  0.6 205.3 %shard_map.67 = (f32[2,32,128]{2,1,0:T(8,128)}, f32[2,32,128]{2,1,0:T(8,128)}, f32[8192,256]{1,0:T(8,128)}, bf16[8192,128]{1,0:T(8,128)(2,1)}) custom-call(bf16[160,8192]{1,0:T(8,128)(2,1)} %x_ref.1, bf16[2,640,128]{2,1,0:T(8,128)(2,1)} %k_ref.1, bf16[2,8192,128]{2,1,0:T(8,128)(2,1)} %bitcast.7, f32[2,32,128]{2,1,0:T(8,128)} %bitcast.8), custom_call_target="tpu_custom_call" | custom-call | tf_op jit(solution)/shard_map/pallas_call | solution.py:491
  205.9 6.4 %shard_map.68 = (f32[2,32,128]{2,1,0:T(8,128)}, f32[2,32,128]{2,1,0:T(8,128)}, bf16[2,8192,128]{2,1,0:T(8,128)(2,1)}) custom-call(f32[2,32,128]{2,1,0:T(8,128)} %get-tuple-element.10.p_ref, f32[2,32,128]{2,1,0:T(8,128)} %get-tuple-element.11.q_ref, f32[8192,256]{1,0:T(8,128)} %get-tuple-element.12.merged_ref, bf16[8192,128]{1,0:T(8,128)(2,1)} %get-tuple-element.13.bt_ref), custom_call_target="tpu_custom_call" | custom-call | tf_op jit(solution)/shard_map/pallas_call | solution.py:533
